TPU v7x, 32 devices: a whole 2x2x4 slice. The times are simulated.
32 devices in a mesh: ctx: 8 (over z, y), tp: 4 (over x, core).
Axes of the slice: x: 2, y: 2, z: 4, core: 2. Of those that a mesh axis runs over, the one named last changes fastest.
Arguments:
- queries: bfloat16 [1024, 4096], P('ctx', 'tp'), may hold values from -64 to 64
- keys: bfloat16 [1024, 1024], P('ctx', 'tp'), may hold values from -4 to 4
- values: bfloat16 [1024, 1024], P('ctx', 'tp'), may hold values from -6 to 6
- grad_out: bfloat16 [1024, 4096], P('ctx', 'tp'), may hold values from -6 to 6
- out_weight: bfloat16 [4096, 4096], P(None, 'tp'), may hold values from -0.09375 to 0.09375
- segments: int32 [1024], P('ctx'), may hold values from 0 to 1, as said below
Outputs:
- query_grad: bfloat16 [1024, 4096], P('ctx', 'tp')
- key_gradient: bfloat16 [1024, 1024], P('ctx', 'tp')
- value_gradient: bfloat16 [1024, 1024], P('ctx', 'tp')
Inputs may be any that keep to these rules, and one draw needn't show every extreme that they name: `segments`: document numbers never fall along the tokens, start at 0, and every document starts at a multiple of 8 tokens; there are exactly 2 documents.
All inputs are finite; a program needn't handle non-finite values.
Results may differ from a plain program's by a relative error of at most 0.015.
Values may be sent and summed in bfloat16 or wider, within the bound.
A program may use at most 128 MiB of HBM per device.

v0:
```python
import jax
import jax.numpy as jnp
from jax import lax
from jax.sharding import PartitionSpec as P

QUERY_HEADS = 32
KEY_VALUE_HEADS = 8
HEAD_SIZE = 128


def per_device(queries, keys, values, grad_out, out_weight, segments):
    rows = queries.shape[0]
    groups = keys.shape[1] // HEAD_SIZE
    group_ratio = QUERY_HEADS // KEY_VALUE_HEADS
    scale = HEAD_SIZE ** (-0.5)
    first = lax.axis_index("ctx") * rows
    qpos = first + jnp.arange(rows, dtype=jnp.int32)
    last_pos = first + rows - 1
    first_seg = segments[0]
    upstream_wide = jnp.dot(
        lax.all_gather(grad_out, "tp", axis=1, tiled=True),
        out_weight,
        preferred_element_type=jnp.float32,
    )
    upstream = upstream_wide.astype(jnp.bfloat16).reshape(rows, groups, group_ratio, HEAD_SIZE)
    query_four = queries.reshape(rows, groups, group_ratio, HEAD_SIZE)
    all_keys, all_values, all_segs = (
        lax.all_gather(keys, "ctx", axis=0, tiled=True),
        lax.all_gather(values, "ctx", axis=0, tiled=True),
        lax.all_gather(segments, "ctx", axis=0, tiled=True),
    )
    total = all_keys.shape[0]
    width = min(512, total)
    blocks = total // width

    def block_at(index):
        start = index * width
        key_blk = lax.dynamic_slice_in_dim(all_keys, start, width, 0).reshape(
            width, groups, HEAD_SIZE
        )
        value_blk = lax.dynamic_slice_in_dim(all_values, start, width, 0).reshape(
            width, groups, HEAD_SIZE
        )
        seg_blk = lax.dynamic_slice_in_dim(all_segs, start, width, 0)
        kpos = start + jnp.arange(width, dtype=jnp.int32)
        allowed = (kpos[None, :] <= qpos[:, None]) & (seg_blk[None, :] == segments[:, None])
        needed = (start <= last_pos) & (seg_blk[width - 1] >= first_seg)
        return (start, key_blk, value_blk, allowed, needed)

    def block_scores(key_blk, value_blk, allowed):
        scores = (
            jnp.einsum("qgrd,kgd->grqk", query_four, key_blk, preferred_element_type=jnp.float32)
            * scale
        )
        scores = jnp.where(allowed[None, None], scores, jnp.float32(-1e30))
        dprobs = jnp.einsum(
            "qgrd,kgd->grqk", upstream, value_blk, preferred_element_type=jnp.float32
        )
        return (scores, dprobs)

    def statistics(index, carry):
        start, key_blk, value_blk, allowed, needed = block_at(index)

        def statistics_update(state):
            top_old, mass, weighted = state
            scores, dprobs = block_scores(key_blk, value_blk, allowed)
            top_new = jnp.maximum(top_old, jnp.max(scores, axis=-1))
            probs = jnp.where(allowed[None, None], jnp.exp(scores - top_new[..., None]), 0.0)
            factor = jnp.exp(top_old - top_new)
            mass = mass * factor + jnp.sum(probs, axis=-1)
            weighted = weighted * factor + jnp.sum(probs * dprobs, axis=-1)
            return (top_new, mass, weighted)

        return lax.cond(needed, statistics_update, lambda state: state, carry)

    start_state = (
        jnp.full((groups, group_ratio, rows), -1e30, jnp.float32),
        jnp.zeros((groups, group_ratio, rows), jnp.float32),
        jnp.zeros((groups, group_ratio, rows), jnp.float32),
    )
    top, mass, weighted = lax.fori_loop(0, blocks, statistics, start_state)
    lse = top + jnp.log(mass)
    delta = weighted / mass

    def gradients(index, carry):
        start, key_blk, value_blk, allowed, needed = block_at(index)

        def gradients_update(state):
            query_acc, key_acc, value_acc = state
            scores, dprobs = block_scores(key_blk, value_blk, allowed)
            probs = jnp.where(allowed[None, None], jnp.exp(scores - lse[..., None]), 0.0)
            dscores = probs * (dprobs - delta[..., None])
            probs_low = probs.astype(jnp.bfloat16)
            dscores_low = dscores.astype(jnp.bfloat16)
            query_acc = query_acc + jnp.einsum(
                "grqk,kgd->qgrd", dscores_low, key_blk, preferred_element_type=jnp.float32
            )
            key_term = (
                jnp.einsum(
                    "grqk,qgrd->kgd", dscores_low, query_four, preferred_element_type=jnp.float32
                )
                * scale
            )
            value_term = jnp.einsum(
                "grqk,qgrd->kgd", probs_low, upstream, preferred_element_type=jnp.float32
            )
            key_acc = lax.dynamic_update_slice_in_dim(
                key_acc, key_term.reshape(width, groups * HEAD_SIZE), start, 0
            )
            value_acc = lax.dynamic_update_slice_in_dim(
                value_acc, value_term.reshape(width, groups * HEAD_SIZE), start, 0
            )
            return (query_acc, key_acc, value_acc)

        return lax.cond(needed, gradients_update, lambda state: state, carry)

    empty_terms = jnp.zeros((total, groups * HEAD_SIZE), jnp.float32)
    grad_state = (
        jnp.zeros((rows, groups, group_ratio, HEAD_SIZE), jnp.float32),
        empty_terms,
        empty_terms,
    )
    query_acc, key_terms, value_terms = lax.fori_loop(0, blocks, gradients, grad_state)
    query_grad = (
        (query_acc * scale).reshape(rows, groups * group_ratio * HEAD_SIZE).astype(jnp.bfloat16)
    )
    key_sum, value_sum = (
        lax.psum_scatter(key_terms, "ctx", scatter_dimension=0, tiled=True),
        lax.psum_scatter(value_terms, "ctx", scatter_dimension=0, tiled=True),
    )
    return (query_grad, key_sum.astype(jnp.bfloat16), value_sum.astype(jnp.bfloat16))


def solution(mesh):
    in_specs = (
        P("ctx", "tp"),
        P("ctx", "tp"),
        P("ctx", "tp"),
        P("ctx", "tp"),
        P(None, "tp"),
        P("ctx"),
    )
    out_specs = (P("ctx", "tp"), P("ctx", "tp"), P("ctx", "tp"))
    return jax.shard_map(
        per_device, mesh=mesh, in_specs=in_specs, out_specs=out_specs, check_vma=False
    )
```

profile of v0, /device:TPU:0, one launch (start us, length us, event | category | flops | bytes accessed | tf_op | source)
XLA Modules:
  0.0 257.5 jit_solution(11375143610156960663)
XLA Ops:
  7.2 0.0 all-gather.3.cloned.1.call-start
  7.2 0.7 all-gather.3.cloned.1.call-update
  7.9 0.0 reduce-scatter.3.cloned.1.call-start
  7.9 0.9 copy.50
  8.9 1.8 copy.51
  10.7 1.1 copy.53
  11.8 1.0 copy.52
  12.8 22.3 %all-gather = s32[8,1,128]{2,1,0:T(1,128)S(1)} all-gather(s32[1,1,128]{2,1,0:T(1,128)} %bitcast.130), channel_id=1, replica_groups=mesh['ctx'=8,'tp'=4] {'ctx'}, dimensions={0}, use_global_device_ids=true | all-gather | bytes 4608 | tf_op jit(solution)/shard_map/all_gather | solution.py:30
  35.1 27.9 %all_gather.13 = bf16[1024,256]{0,1:T(8,128)(2,1)S(1)} all-gather(bf16[128,256]{0,1:T(8,128)(2,1)S(1)} %copy.50), channel_id=1, replica_groups=mesh['ctx'=8,'tp'=4] {'ctx'}, dimensions={0}, use_global_device_ids=true | all-gather | bytes 589824 | tf_op jit(solution)/shard_map/all_gather | solution.py:28
  63.1 27.0 %all_gather.14 = bf16[1024,256]{0,1:T(8,128)(2,1)S(1)} all-gather(bf16[128,256]{0,1:T(8,128)(2,1)S(1)} %copy.52), channel_id=1, replica_groups=mesh['ctx'=8,'tp'=4] {'ctx'}, dimensions={0}, use_global_device_ids=true | all-gather | bytes 589824 | tf_op jit(solution)/shard_map/all_gather | solution.py:29
  90.1 5.0 %convolution_convert_fusion = bf16[128,1024]{1,0:T(8,128)(2,1)S(1)} fusion(bf16[128,4096]{1,0:T(8,128)(2,1)} %all-gather.3.cloned.1.call-done, bf16[4096,1024]{1,0:T(8,128)(2,1)} %param.18), kind=kOutput, calls=%fused_computation.36 | convolution fusion | flops 1073872896 | bytes 9699328 | tf_op jit(solution)/shard_map/dot_general | solution.py:20
  95.1 0.2 reshape.78
  95.3 0.2 copy.55
  95.6 5.0 %while.36 = (s32[]{:T(128)}, f32[2,4,128]{2,1,0:T(4,128)S(1)}, f32[2,4,128]{2,1,0:T(4,128)S(1)}, f32[2,4,128]{2,1,0:T(4,128)S(1)}, s32[]{:T(128)}, /*index=5*/s3...) while((s32[]{:T(128)}, f32[2,4,128]{2,1,0:T(4,128)S(1)}, ...), condition=%wide.region_6.7_spmd.clone, body=%wide.region_0.6_spmd.clone.sunk | while | flops 275975808 | bytes 8741805 | solution.py:81
  95.6 0.1 dynamic_slice.70
  95.7 0.6 slice.22
  97.0 2.2 conditional.6
  97.1 0.2 compare_and_fusion
  97.3 0.5 fusion.5
  97.8 0.8 fusion.4
  98.7 0.5 fusion.6
  99.2 0.1 dynamic_slice.70
  99.3 0.6 slice.22
  100.7 1.2 broadcast_in_dim.89
  101.8 1.1 broadcast_in_dim.89.clone
  103.0 8.9 %while.37 = (s32[]{:T(128)}, f32[128,2,4,128]{3,0,2,1:T(8,128)S(1)}, f32[1024,256]{0,1:T(8,128)}, f32[1024,256]{0,1:T(8,128)}, s32[]{:T(128)}, /*index=5*/s32[10...) while((s32[]{:T(128)}, ...), condition=%wide.region_10.11_spmd.clone, body=%wide.region_7.10_spmd.clone.sunk | while | flops 675742336 | bytes 16671735 | solution.py:123
  103.0 0.1 dynamic_slice.71
  103.0 0.6 slice.23
  104.3 6.2 %conditional.7 = ((f32[128,2,4,128]{3,0,2,1:T(8,128)S(1)}, f32[1024,256]{0,1:T(8,128)}, f32[1024,256]{0,1:T(8,128)})) conditional(s32[]{:T(128)} %convert_element_type.54, (f32[128,2,4,128]{3,0,2,1:T(8,128)S(1)}, f32[1024,256]{0,1:T(8,128)}, f32[1024,256]{0,1:T(8,128)}) %tuple.106, (s32[]{:T(128)}, s32[1,512]{1,0:T(1,128)S(1)}, s32[]{:T(128)}, ...), branch_computations={%region_8.8_spmd, %region_9.9_spmd} | conditional | flops 675742336 | bytes 16664662 | solution.py:115
  104.4 0.2 compare_and_fusion.1
  104.6 1.7 fusion.11
  106.3 0.5 fusion.8
  106.8 0.6 fusion.13
  107.5 0.5 fusion.14
  107.9 1.4 fusion.12
  109.4 1.1 constant_dynamic-update-slice_fusion
  110.5 0.1 dynamic_slice.71
  110.5 0.6 slice.23
  111.8 2.5 copy.57
  114.4 0.0 reduce-scatter.5.cloned.1.call-start
  114.4 2.6 %copy.58 = f32[1024,256]{1,0:T(8,128)} copy(f32[1024,256]{0,1:T(8,128)} %get-tuple-element.743) | data formatting | bytes 2097152 | tf_op jit(solution)/shard_map/while | solution.py:123
  117.1 0.1 multiply_convert_fusion
  117.1 0.2 copy.56
  117.3 0.9 convert_element_type.41
  118.2 65.1 %reduce-scatter.3.cloned.1.call-done = f32[128,256]{1,0:T(8,128)} async-done(((f32[1024,256]{1,0:T(8,128)}), f32[128,256]{1,0:T(8,128)}) %reduce-scatter.3.cloned.1.call-update) | async-done | bytes 131088 | tf_op jit(solution)/shard_map/reduce_scatter | solution.py:128
  183.3 1.5 convert_element_type.42
  184.8 64.7 %reduce-scatter.5.cloned.1.call-done = f32[128,256]{1,0:T(8,128)} async-done(((f32[1024,256]{1,0:T(8,128)}), f32[128,256]{1,0:T(8,128)}) %reduce-scatter.5.cloned.1.call-update) | async-done | bytes 131088 | tf_op jit(solution)/shard_map/reduce_scatter | solution.py:129
  249.5 1.5 convert_element_type.43
  (31 shorter events, 0.3 us)
Async XLA Ops:
  7.2 82.9 %all-gather.3.cloned.1.call-start = ((), (), s32[]{:S(2)}) async-start(), calls=%async_computation.2 | async-start | bytes 1310720 | tf_op jit(solution)/shard_map/all_gather | solution.py:21
  7.9 175.4 %reduce-scatter.3.cloned.1.call-start = ((), (), s32[]{:S(2)}) async-start(), calls=%async_computation.3 | async-start | bytes 1179648 | tf_op jit(solution)/shard_map/reduce_scatter | solution.py:128
  90.1 5.5 %copy-start = (s32[128]{0:T(128)S(1)}, s32[128]{0:T(128)}, u32[]{:S(2)}) copy-start(s32[128]{0:T(128)} %param.19) | copy-start | bytes 1540
  114.4 135.1 %reduce-scatter.5.cloned.1.call-start = ((), (), s32[]{:S(2)}) async-start(), calls=%async_computation.4 | async-start | bytes 1179648 | tf_op jit(solution)/shard_map/reduce_scatter | solution.py:129
Sparse Core Ops, SparseCore 0:
  9.6 19.4 all-gather.2
  114.5 68.7 reduce-scatter.2
  187.1 62.3 reduce-scatter.4
where the time goes:
time: 258 us
  waiting for transfers between devices  130 us (50%)
  blocking collectives  77.3 us (30%)
  local copies, waits for them, and re-layouts  17.7 us (7%)
  between operations  13.9 us (5%)
  matrix products  11.1 us (4%)
  other arithmetic  4.11 us (2%)
  loops' own time  2.94 us (1%)
    reduce_scatter x1, waiting for transfers between devices, per_device(): lax.psum_scatter(key_terms, 'ctx', scatter_dimension=0, tiled=True)  65.1 us
    reduce_scatter x1, waiting for transfers between devices, per_device(): lax.psum_scatter(value_terms, 'ctx', scatter_dimension=0, tiled=True)  64.7 us
    all_gather x1, blocking collectives, per_device(): lax.all_gather(keys, 'ctx', axis=0, tiled=True)  27.9 us
    all_gather x1, blocking collectives, per_device(): lax.all_gather(values, 'ctx', axis=0, tiled=True)  27 us
    all_gather x1, blocking collectives, per_device(): lax.all_gather(segments, 'ctx', axis=0, tiled=True)  22.3 us
  transfers between devices with their start and end apart: 3, of which 2 were waited for; matrix products, arithmetic and copies ran while one was open for 4% of the time, Pallas kernels for 0%

commit v1 on v0

v1 whole, which is shorter than its diff:
```python
import functools

import jax
import jax.numpy as jnp
from jax import lax
from jax.experimental import pallas as pl
from jax.experimental.pallas import tpu as pltpu
from jax.sharding import PartitionSpec as P

QUERY_HEADS = 32
KEY_VALUE_HEADS = 8
HEAD_SIZE = 128
RATIO = QUERY_HEADS // KEY_VALUE_HEADS
SEG_ROWS = 16
LOG2E = 1.4426950408889634
MESH = pl.DeviceIdType.MESH
F32 = jnp.float32
BF16 = jnp.bfloat16


def dot(a, b, ca, cb):
    return lax.dot_general(a, b, (((ca,), (cb,)), ((), ())), preferred_element_type=F32)


def kernel(
    stages, q_in, k_in, v_in, g_in, w_hbm, seg_in,
    q_out, k_out, v_out,
    wbuf, gbuf, acc, kv, ky, qbuf, ubuf, usend, mst, lst, wst, ones,
    dq, dqs, dqr, own, rs, ret, fins, finr,
    w_sem, gx_s, gx_r, gc_s, gc_r, gf_s, gf_r, kv_s, kv_r, ret_s, ret_r,
    misc_s, misc_r, fin_s, fin_r,
):
    rows = k_in.shape[0]
    pair = 2 * rows
    hs = HEAD_SIZE
    gw = RATIO * hs
    half = g_in.shape[1] // 2
    scale = HEAD_SIZE ** -0.5
    ctx = lax.axis_index("ctx")
    tp = lax.axis_index("tp")
    s, y = ctx // 2, ctx % 2
    z = 1 - y
    x, c = tp // 2, tp % 2
    sib = (2 * s + z, tp)
    down = (2 * lax.rem(s + 1, stages) + y, tp)
    up = (2 * lax.rem(s + stages - 1, stages) + y, tp)
    xnb = (ctx, 2 * (1 - x) + c)
    core = (ctx, 2 * x + 1 - c)
    t_own, t_core, t_x, t_f = tp, 2 * x + 1 - c, 2 * (1 - x) + c, 2 * (1 - x) + 1 - c

    def remote(src, dst, a, b, dev):
        return pltpu.make_async_remote_copy(
            src_ref=src, dst_ref=dst, send_sem=a, recv_sem=b, device_id=dev, device_id_type=MESH
        )

    def w_copy(t, h):
        i = 2 * t + h
        return pltpu.make_async_copy(w_hbm.at[pl.ds(i * half, half)], wbuf.at[i], w_sem.at[i])

    for t in (t_own, t_core, t_x, t_f):
        for h in range(2):
            w_copy(t, h).start()

    def fill(dst, g):
        cols = pl.ds(pl.multiple_of(g * hs, hs), hs)
        dst[0:rows, :] = k_in[:, cols]
        dst[rows : 2 * rows, :] = v_in[:, cols]
        dst[2 * rows :, :] = jnp.broadcast_to(seg_in[...].astype(F32), (SEG_ROWS, rows)).astype(BF16)

    fill(kv.at[s, y], y)
    fill(ky, z)

    barrier = pltpu.get_barrier_semaphore()
    for dev in (sib, down, up, xnb, core):
        pl.semaphore_signal(barrier, inc=1, device_id=dev, device_id_type=MESH)
    pl.semaphore_wait(barrier, 5)

    def chain(k, p):
        return remote(kv.at[k, p], kv.at[k, p], kv_s.at[k, p], kv_r.at[k, p], down)

    ky_copy = remote(ky, kv.at[s, y], misc_s.at[0], misc_r.at[0], sib)
    q_copy = remote(
        q_in.at[:, pl.ds(pl.multiple_of(z * gw, gw), gw)], qbuf.at[y], misc_s.at[1], misc_r.at[1], sib
    )
    u_copy = remote(usend, ubuf.at[y], misc_s.at[2], misc_r.at[2], sib)
    dq_copy = remote(dqs, dqr, misc_s.at[3], misc_r.at[3], sib)
    gx = [
        remote(g_in.at[:, h * half : (h + 1) * half], gbuf.at[t_own, h], gx_s.at[h], gx_r.at[h], xnb)
        for h in range(2)
    ]
    gc = [
        remote(g_in.at[:, h * half : (h + 1) * half], gbuf.at[t_own, h], gc_s.at[h], gc_r.at[h], core)
        for h in range(2)
    ]
    gf = [remote(gbuf.at[t_x, h], gbuf.at[t_x, h], gf_s.at[h], gf_r.at[h], core) for h in range(2)]
    last = s == stages - 1

    ky_copy.start()
    gx[0].start()

    @pl.when(jnp.logical_not(last))
    def _():
        chain(s, y).start()

    gx[1].start()
    gc[0].start()
    gc[1].start()
    q_copy.start()

    qbuf[y] = q_in[:, pl.ds(pl.multiple_of(y * gw, gw), gw)]

    def product(left, t, h):
        w_copy(t, h).wait()
        return dot(left, wbuf[2 * t + h], 1, 0)

    acc[...] = product(g_in[:, 0:half], t_own, 0)
    acc[...] += product(g_in[:, half:], t_own, 1)

    ky_copy.wait_recv()

    @pl.when(jnp.logical_not(last))
    def _():
        chain(s, z).start()

    for h in range(2):
        gc[h].wait_recv()
        acc[...] += product(gbuf[t_core, h], t_core, h)
    gx[0].wait_recv()
    gf[0].start()
    acc[...] += product(gbuf[t_x, 0], t_x, 0)

    def arrive(k):
        for p in range(2):
            chain(k, p).wait_recv()

            @pl.when(jnp.logical_not(last))
            def _():
                chain(k, p).start()

    @pl.when(s >= 1)
    def _():
        arrive(s - 1)

    gx[1].wait_recv()
    gf[1].start()
    acc[...] += product(gbuf[t_x, 1], t_x, 1)
    for h in range(2):
        gf[h].wait_recv()
        acc[...] += product(gbuf[t_f, h], t_f, h)
    usend[...] = acc[:, pl.ds(pl.multiple_of(z * gw, gw), gw)].astype(BF16)
    u_copy.start()
    ubuf[y] = acc[:, pl.ds(pl.multiple_of(y * gw, gw), gw)].astype(BF16)

    @pl.when(jnp.logical_not(last))
    def _():
        def body(i, carry):
            arrive(s - 2 - i)
            return carry

        lax.fori_loop(0, s - 1, body, 0)

    q_copy.wait_recv()
    u_copy.wait_recv()

    mst[...] = jnp.full(mst.shape, -1e20, F32)
    lst[...] = jnp.zeros(lst.shape, F32)
    wst[...] = jnp.zeros(wst.shape, F32)
    ones[...] = jnp.zeros(ones.shape, F32)
    dq[...] = jnp.zeros(dq.shape, F32)

    def heads(ref, r):
        return ref[:, :, r * hs : (r + 1) * hs].reshape(pair, hs)

    def block(k):
        keys = kv[k, :, 0:rows, :].reshape(pair, hs)
        values = kv[k, :, rows : 2 * rows, :].reshape(pair, hs)
        begin = (s + 1) * pair - ones[0:1, :].astype(jnp.int32)
        qpos = s * pair + lax.broadcasted_iota(jnp.int32, (1, pair), 1)
        low = jnp.where(qpos < begin, 0, begin)
        kpos = k * pair + lax.broadcasted_iota(jnp.int32, (pair, pair), 0)
        return keys, values, (kpos <= qpos) & (kpos >= low)

    def scores(keys, values, allowed, r):
        sc = dot(keys, heads(qbuf, r), 1, 1) * (scale * LOG2E)
        return jnp.where(allowed, sc, -1e30), dot(values, heads(ubuf, r), 1, 1)

    def statistics(i, carry):
        k = s - i

        @pl.when(last & (k < s - 1))
        def _():
            for p in range(2):
                chain(k, p).wait_recv()

        seg = kv[k, :, 2 * rows :, :].astype(F32).reshape(2 * SEG_ROWS, rows)
        count = jnp.sum(jnp.sum(seg, axis=0, keepdims=True), axis=1, keepdims=True) * (1.0 / SEG_ROWS)
        ones[...] += jnp.broadcast_to(count, ones.shape)
        keys, values, allowed = block(k)
        for r in range(RATIO):
            sc, dp = scores(keys, values, allowed, r)
            old = mst[r : r + 1, :]
            new = jnp.maximum(old, jnp.max(sc, axis=0, keepdims=True))
            pr = jnp.exp2(sc - new)
            factor = jnp.exp2(old - new)
            mst[r : r + 1, :] = new
            lst[r : r + 1, :] = lst[r : r + 1, :] * factor + jnp.sum(pr, axis=0, keepdims=True)
            wst[r : r + 1, :] = wst[r : r + 1, :] * factor + jnp.sum(pr * dp, axis=0, keepdims=True)
        return carry

    lax.fori_loop(0, s + 1, statistics, 0)
    mst[...] = mst[...] + jnp.log2(lst[...])
    wst[...] = wst[...] / lst[...]

    def back(k, p):
        return remote(rs.at[k, p], ret.at[k, p], ret_s.at[k, p], ret_r.at[k, p], up)

    def gradients(k, carry):
        keys, values, allowed = block(k)
        dk = jnp.zeros((pair, hs), F32)
        dv = jnp.zeros((pair, hs), F32)
        for r in range(RATIO):
            sc, dp = scores(keys, values, allowed, r)
            pr = jnp.exp2(sc - mst[r : r + 1, :])
            ds = (pr * (dp - wst[r : r + 1, :])).astype(BF16)
            dv += dot(pr.astype(BF16), heads(ubuf, r), 1, 0)
            dk += dot(ds, heads(qbuf, r), 1, 0)
            dq[r] += dot(ds, keys, 0, 0)
        own[k, 0] = dk * scale
        own[k, 1] = dv

        @pl.when(last & (k < s))
        def _():
            for p in range(2):
                rs[k, p] = own[k, p].astype(BF16)
                back(k, p).start()

        return carry

    lax.fori_loop(0, s + 1, gradients, 0)

    for r in range(RATIO):
        dqs[:, r * hs : (r + 1) * hs] = (
            dq[r, pl.ds(pl.multiple_of(z * rows, rows), rows), :] * scale
        ).astype(BF16)
    dq_copy.start()
    for r in range(RATIO):
        q_out[:, pl.ds(pl.multiple_of(y * gw, gw) + r * hs, hs)] = (
            dq[r, pl.ds(pl.multiple_of(y * rows, rows), rows), :] * scale
        ).astype(BF16)

    @pl.when(jnp.logical_not(last))
    def _():
        def body(k, carry):
            for p in range(2):
                back(k, p).wait_recv()
                rs[k, p] = (own[k, p] + ret[k, p].astype(F32)).astype(BF16)
                back(k, p).start()
            return carry

        lax.fori_loop(0, s, body, 0)
        for p in range(2):
            back(s, p).wait_recv()
            own[s, p] = own[s, p] + ret[s, p].astype(F32)

    fin = [remote(fins.at[p], finr.at[p], fin_s.at[p], fin_r.at[p], sib) for p in range(2)]
    for p in range(2):
        fins[p] = own[s, p, pl.ds(pl.multiple_of(z * rows, rows), rows), :].astype(BF16)
        fin[p].start()
    mine = pl.ds(pl.multiple_of(y * hs, hs), hs)
    theirs = pl.ds(pl.multiple_of(z * hs, hs), hs)
    for p, out in enumerate((k_out, v_out)):
        out[:, mine] = own[s, p, pl.ds(pl.multiple_of(y * rows, rows), rows), :].astype(BF16)
    dq_copy.wait_recv()
    q_out[:, pl.ds(pl.multiple_of(z * gw, gw), gw)] = dqr[...]
    for p, out in enumerate((k_out, v_out)):
        fin[p].wait_recv()
        out[:, theirs] = finr[p]

    for copy in (ky_copy, q_copy, u_copy, dq_copy, *gx, *gc, *gf, *fin):
        copy.wait_send()

    @pl.when(jnp.logical_not(last))
    def _():
        def body(k, carry):
            for p in range(2):
                chain(k, p).wait_send()
            return carry

        lax.fori_loop(0, s + 1, body, 0)

    def drain(k, carry):
        for p in range(2):
            back(k, p).wait_send()
        return carry

    lax.fori_loop(0, s, drain, 0)


def per_device(stages, queries, keys, values, grad_out, out_weight, segments):
    rows, wide = queries.shape
    depth = grad_out.shape[1]
    pair, hs, gw = 2 * rows, HEAD_SIZE, RATIO * HEAD_SIZE
    vmem = pl.BlockSpec(memory_space=pltpu.VMEM)
    dma = pltpu.SemaphoreType.DMA
    return pl.pallas_call(
        functools.partial(kernel, stages),
        out_shape=(
            jax.ShapeDtypeStruct(queries.shape, BF16),
            jax.ShapeDtypeStruct(keys.shape, BF16),
            jax.ShapeDtypeStruct(values.shape, BF16),
        ),
        in_specs=[vmem, vmem, vmem, vmem, pl.BlockSpec(memory_space=pl.ANY), vmem],
        out_specs=(vmem, vmem, vmem),
        scratch_shapes=[
            pltpu.VMEM((8, depth // 2, wide), BF16),
            pltpu.VMEM((4, 2, rows, depth // 2), BF16),
            pltpu.VMEM((rows, wide), F32),
            pltpu.VMEM((stages, 2, pair + SEG_ROWS, hs), BF16),
            pltpu.VMEM((pair + SEG_ROWS, hs), BF16),
            pltpu.VMEM((2, rows, gw), BF16),
            pltpu.VMEM((2, rows, gw), BF16),
            pltpu.VMEM((rows, gw), BF16),
            pltpu.VMEM((RATIO, pair), F32),
            pltpu.VMEM((RATIO, pair), F32),
            pltpu.VMEM((RATIO, pair), F32),
            pltpu.VMEM((8, pair), F32),
            pltpu.VMEM((RATIO, pair, hs), F32),
            pltpu.VMEM((rows, gw), BF16),
            pltpu.VMEM((rows, gw), BF16),
            pltpu.VMEM((stages, 2, pair, hs), F32),
            pltpu.VMEM((stages, 2, pair, hs), BF16),
            pltpu.VMEM((stages, 2, pair, hs), BF16),
            pltpu.VMEM((2, rows, hs), BF16),
            pltpu.VMEM((2, rows, hs), BF16),
            dma((8,)),
            dma((2,)), dma((2,)), dma((2,)), dma((2,)), dma((2,)), dma((2,)),
            dma((stages, 2)), dma((stages, 2)), dma((stages, 2)), dma((stages, 2)),
            dma((4,)), dma((4,)), dma((2,)), dma((2,)),
        ],
        compiler_params=pltpu.CompilerParams(
            collective_id=0, has_side_effects=True, vmem_limit_bytes=56 * 1024 * 1024
        ),
        name="attention_backward",
    )(queries, keys, values, grad_out, out_weight, segments.reshape(1, rows))


def solution(mesh):
    in_specs = (
        P("ctx", "tp"),
        P("ctx", "tp"),
        P("ctx", "tp"),
        P("ctx", "tp"),
        P(None, "tp"),
        P("ctx"),
    )
    out_specs = (P("ctx", "tp"), P("ctx", "tp"), P("ctx", "tp"))
    return jax.shard_map(
        functools.partial(per_device, mesh.shape["ctx"] // 2),
        mesh=mesh, in_specs=in_specs, out_specs=out_specs, check_vma=False,
    )
```

time: 258 us -> 45.5 us (0.18)
  waiting for transfers between devices: 130 us -> 0 us
  blocking collectives: 77.3 us -> 0 us
  Pallas kernels: 0 us -> 40 us
  between operations: 13.9 us -> 0.64 us
  local copies, waits for them, and re-layouts: 17.7 us -> 4.61 us
  matrix products: 11.1 us -> 0 us
  other arithmetic: 4.11 us -> 0 us
  loops' own time: 2.94 us -> 0 us
    reduce_scatter x2 -> x0, waiting for transfers between devices: 130 us -> none  [the longest x1 65.1 us: per_device(): lax.psum_scatter(key_terms, 'ctx', scatter_dimension=0, tiled=True)]
    all_gather x3 -> x0, blocking collectives: 77.3 us -> none  [the longest x1 27.9 us: per_device(): lax.all_gather(keys, 'ctx', axis=0, tiled=True)]
    pallas_call x0 -> x1, Pallas kernels: none -> 40 us  [per_device(): pl.pallas_call(functools.partial(kernel, stages), out_shape=(jax.ShapeDty...]
    dot_general x8 -> x0, matrix products: 11.1 us -> none  [the longest x1 4.98 us: per_device(): jnp.dot(lax.all_gather(grad_out, 'tp', axis=1, tiled=True), out_weight, p...]
    while x2 -> x0, local copies, waits for them, and re-layouts: 5.12 us -> none  [per_device(): lax.fori_loop(0, blocks, gradients, grad_state)]
    convert_element_type x3 -> x0, other arithmetic: 3.14 us -> none  [the longest x1 1.54 us: per_device(): value_sum.astype(jnp.bfloat16)]
    another operation x6 -> x0, loops' own time: 2.94 us -> none  [the longest x1 1.4 us: per_device(): top, mass, weighted = lax.fori_loop(0, blocks, statistics, start_state)]
  transfers between devices with their start and end apart: 3 -> 0, of which waited for: 2 -> 0; matrix products, arithmetic and copies ran while one was open for 4% -> 0% of each run, Pallas kernels for 0% -> 0%
where the time goes in v1:
time: 45.5 us; the launch traced here: 45.3 us
  Pallas kernels  40 us (88%)
  local copies, waits for them, and re-layouts  4.61 us (10%)
  between operations  0.64 us (1%)
    pallas_call x1, Pallas kernels, per_device(): pl.pallas_call(functools.partial(kernel, stages), out_shape=(jax.ShapeDty...  40 us
    unnamed x3, local copies, waits for them, and re-layouts  4.61 us

profile of v1, /device:TPU:0, one launch (start us, length us, event | category | flops | bytes accessed | tf_op | source)
XLA Modules:
  0.0 45.3 jit_solution(2328329722089975026)
XLA Ops:
  0.6 40.0 %attention_backward.1 = (bf16[128,1024]{1,0:T(8,128)(2,1)}, bf16[128,256]{1,0:T(8,128)(2,1)}, bf16[128,256]{1,0:T(8,128)(2,1)}) custom-call(bf16[128,1024]{1,0:T(8,128)(2,1)} %q_in.1, bf16[128,256]{1,0:T(8,128)(2,1)} %k_in.1, bf16[128,256]{1,0:T(8,128)(2,1)} %v_in.1, bf16[128,1024]{1,0:T(8,128)(2,1)} %g_in.1, bf16[4096,1024]{1,0:T(8,128)(2,1)} %w_hbm.1, ...), custom_call_target="tpu_custom_call" | custom-call | tf_op jit(solution)/shard_map/attention_backward/pallas_call | solution.py:305
  40.6 1.7 %copy.12 = bf16[128,1024]{1,0:T(8,128)(2,1)} copy(bf16[128,1024]{1,0:T(8,128)(2,1)} %get-tuple-element.6) | data formatting | bytes 524288
  42.3 1.5 %copy.13 = bf16[128,256]{1,0:T(8,128)(2,1)} copy(bf16[128,256]{1,0:T(8,128)(2,1)} %get-tuple-element.7) | data formatting | bytes 131072
  43.8 1.5 %copy.14 = bf16[128,256]{1,0:T(8,128)(2,1)} copy(bf16[128,256]{1,0:T(8,128)(2,1)} %get-tuple-element.8) | data formatting | bytes 131072

commit v2 on v1

--- a/solution.py
+++ b/solution.py
@@ -12,6 +12,7 @@
 HEAD_SIZE = 128
 RATIO = QUERY_HEADS // KEY_VALUE_HEADS
 SEG_ROWS = 16
+KEPT_STAGES = 8
 LOG2E = 1.4426950408889634
 MESH = pl.DeviceIdType.MESH
 F32 = jnp.float32
@@ -25,7 +26,7 @@
 def kernel(
     stages, q_in, k_in, v_in, g_in, w_hbm, seg_in,
     q_out, k_out, v_out,
-    wbuf, gbuf, acc, kv, ky, qbuf, ubuf, usend, mst, lst, wst, ones,
+    wbuf, gbuf, acc, kv, ky, qbuf, ubuf, usend, mst, lst, wst, ones, ot, kept,
     dq, dqs, dqr, own, rs, ret, fins, finr,
     w_sem, gx_s, gx_r, gc_s, gc_r, gf_s, gf_r, kv_s, kv_r, ret_s, ret_r,
     misc_s, misc_r, fin_s, fin_r,
@@ -34,6 +35,7 @@
     pair = 2 * rows
     hs = HEAD_SIZE
     gw = RATIO * hs
+    keep = stages <= KEPT_STAGES
     half = g_in.shape[1] // 2
     scale = HEAD_SIZE ** -0.5
     ctx = lax.axis_index("ctx")
@@ -48,6 +50,10 @@
     core = (ctx, 2 * x + 1 - c)
     t_own, t_core, t_x, t_f = tp, 2 * x + 1 - c, 2 * (1 - x) + c, 2 * (1 - x) + 1 - c
 
+    barrier = pltpu.get_barrier_semaphore()
+    for dev in (sib, down, up, xnb, core):
+        pl.semaphore_signal(barrier, inc=1, device_id=dev, device_id_type=MESH)
+
     def remote(src, dst, a, b, dev):
         return pltpu.make_async_remote_copy(
             src_ref=src, dst_ref=dst, send_sem=a, recv_sem=b, device_id=dev, device_id_type=MESH
@@ -70,9 +76,6 @@
     fill(kv.at[s, y], y)
     fill(ky, z)
 
-    barrier = pltpu.get_barrier_semaphore()
-    for dev in (sib, down, up, xnb, core):
-        pl.semaphore_signal(barrier, inc=1, device_id=dev, device_id_type=MESH)
     pl.semaphore_wait(barrier, 5)
 
     def chain(k, p):
@@ -127,7 +130,6 @@
         acc[...] += product(gbuf[t_core, h], t_core, h)
     gx[0].wait_recv()
     gf[0].start()
-    acc[...] += product(gbuf[t_x, 0], t_x, 0)
 
     def arrive(k):
         for p in range(2):
@@ -141,8 +143,14 @@
     def _():
         arrive(s - 1)
 
+    acc[...] += product(gbuf[t_x, 0], t_x, 0)
     gx[1].wait_recv()
     gf[1].start()
+
+    @pl.when((s >= 2) & jnp.logical_not(last))
+    def _():
+        arrive(s - 2)
+
     acc[...] += product(gbuf[t_x, 1], t_x, 1)
     for h in range(2):
         gf[h].wait_recv()
@@ -154,35 +162,36 @@
     @pl.when(jnp.logical_not(last))
     def _():
         def body(i, carry):
-            arrive(s - 2 - i)
+            arrive(s - 3 - i)
             return carry
 
-        lax.fori_loop(0, s - 1, body, 0)
+        lax.fori_loop(0, s - 2, body, 0)
 
     q_copy.wait_recv()
-    u_copy.wait_recv()
 
     mst[...] = jnp.full(mst.shape, -1e20, F32)
     lst[...] = jnp.zeros(lst.shape, F32)
-    wst[...] = jnp.zeros(wst.shape, F32)
+    ot[...] = jnp.zeros(ot.shape, F32)
     ones[...] = jnp.zeros(ones.shape, F32)
     dq[...] = jnp.zeros(dq.shape, F32)
 
     def heads(ref, r):
         return ref[:, :, r * hs : (r + 1) * hs].reshape(pair, hs)
 
+    def pieces(k):
+        return kv[k, :, 0:rows, :].reshape(pair, hs), kv[k, :, rows : 2 * rows, :].reshape(pair, hs)
+
     def block(k):
-        keys = kv[k, :, 0:rows, :].reshape(pair, hs)
-        values = kv[k, :, rows : 2 * rows, :].reshape(pair, hs)
+        keys, values = pieces(k)
         begin = (s + 1) * pair - ones[0:1, :].astype(jnp.int32)
         qpos = s * pair + lax.broadcasted_iota(jnp.int32, (1, pair), 1)
         low = jnp.where(qpos < begin, 0, begin)
         kpos = k * pair + lax.broadcasted_iota(jnp.int32, (pair, pair), 0)
         return keys, values, (kpos <= qpos) & (kpos >= low)
 
-    def scores(keys, values, allowed, r):
+    def scores(keys, allowed, r):
         sc = dot(keys, heads(qbuf, r), 1, 1) * (scale * LOG2E)
-        return jnp.where(allowed, sc, -1e30), dot(values, heads(ubuf, r), 1, 1)
+        return jnp.where(allowed, sc, -1e30)
 
     def statistics(i, carry):
         k = s - i
@@ -196,18 +205,24 @@
         count = jnp.sum(jnp.sum(seg, axis=0, keepdims=True), axis=1, keepdims=True) * (1.0 / SEG_ROWS)
         ones[...] += jnp.broadcast_to(count, ones.shape)
         keys, values, allowed = block(k)
+        turned = values.T
         for r in range(RATIO):
-            sc, dp = scores(keys, values, allowed, r)
+            sc = scores(keys, allowed, r)
+            if keep:
+                kept[k, r] = sc
             old = mst[r : r + 1, :]
             new = jnp.maximum(old, jnp.max(sc, axis=0, keepdims=True))
             pr = jnp.exp2(sc - new)
             factor = jnp.exp2(old - new)
             mst[r : r + 1, :] = new
             lst[r : r + 1, :] = lst[r : r + 1, :] * factor + jnp.sum(pr, axis=0, keepdims=True)
-            wst[r : r + 1, :] = wst[r : r + 1, :] * factor + jnp.sum(pr * dp, axis=0, keepdims=True)
+            ot[r] = ot[r] * factor + dot(turned, pr.astype(BF16), 1, 0)
         return carry
 
     lax.fori_loop(0, s + 1, statistics, 0)
+    u_copy.wait_recv()
+    for r in range(RATIO):
+        wst[r : r + 1, :] = jnp.sum(heads(ubuf, r).astype(F32).T * ot[r], axis=0, keepdims=True)
     mst[...] = mst[...] + jnp.log2(lst[...])
     wst[...] = wst[...] / lst[...]
 
@@ -215,16 +230,21 @@
         return remote(rs.at[k, p], ret.at[k, p], ret_s.at[k, p], ret_r.at[k, p], up)
 
     def gradients(k, carry):
-        keys, values, allowed = block(k)
+        if keep:
+            keys, values = pieces(k)
+        else:
+            keys, values, allowed = block(k)
+        turned = keys.T
         dk = jnp.zeros((pair, hs), F32)
         dv = jnp.zeros((pair, hs), F32)
         for r in range(RATIO):
-            sc, dp = scores(keys, values, allowed, r)
+            sc = kept[k, r] if keep else scores(keys, allowed, r)
+            dp = dot(values, heads(ubuf, r), 1, 1)
             pr = jnp.exp2(sc - mst[r : r + 1, :])
             ds = (pr * (dp - wst[r : r + 1, :])).astype(BF16)
             dv += dot(pr.astype(BF16), heads(ubuf, r), 1, 0)
             dk += dot(ds, heads(qbuf, r), 1, 0)
-            dq[r] += dot(ds, keys, 0, 0)
+            dq[r] += dot(turned, ds, 1, 0)
         own[k, 0] = dk * scale
         own[k, 1] = dv
 
@@ -240,13 +260,13 @@
 
     for r in range(RATIO):
         dqs[:, r * hs : (r + 1) * hs] = (
-            dq[r, pl.ds(pl.multiple_of(z * rows, rows), rows), :] * scale
-        ).astype(BF16)
+            dq[r, :, pl.ds(pl.multiple_of(z * rows, rows), rows)] * scale
+        ).T.astype(BF16)
     dq_copy.start()
     for r in range(RATIO):
         q_out[:, pl.ds(pl.multiple_of(y * gw, gw) + r * hs, hs)] = (
-            dq[r, pl.ds(pl.multiple_of(y * rows, rows), rows), :] * scale
-        ).astype(BF16)
+            dq[r, :, pl.ds(pl.multiple_of(y * rows, rows), rows)] * scale
+        ).T.astype(BF16)
 
     @pl.when(jnp.logical_not(last))
     def _():
@@ -296,13 +316,21 @@
     lax.fori_loop(0, s, drain, 0)
 
 
+def hand_over(a, b, c, x, y, z, sem):
+    copies = [pltpu.make_async_copy(p, q, sem.at[i]) for i, (p, q) in enumerate(((a, x), (b, y), (c, z)))]
+    for copy in copies:
+        copy.start()
+    for copy in copies:
+        copy.wait()
+
+
 def per_device(stages, queries, keys, values, grad_out, out_weight, segments):
     rows, wide = queries.shape
     depth = grad_out.shape[1]
     pair, hs, gw = 2 * rows, HEAD_SIZE, RATIO * HEAD_SIZE
     vmem = pl.BlockSpec(memory_space=pltpu.VMEM)
     dma = pltpu.SemaphoreType.DMA
-    return pl.pallas_call(
+    grads = pl.pallas_call(
         functools.partial(kernel, stages),
         out_shape=(
             jax.ShapeDtypeStruct(queries.shape, BF16),
@@ -324,7 +352,9 @@
             pltpu.VMEM((RATIO, pair), F32),
             pltpu.VMEM((RATIO, pair), F32),
             pltpu.VMEM((8, pair), F32),
-            pltpu.VMEM((RATIO, pair, hs), F32),
+            pltpu.VMEM((RATIO, hs, pair), F32),
+            pltpu.VMEM((stages if stages <= KEPT_STAGES else 1, RATIO, pair, pair), F32),
+            pltpu.VMEM((RATIO, hs, pair), F32),
             pltpu.VMEM((rows, gw), BF16),
             pltpu.VMEM((rows, gw), BF16),
             pltpu.VMEM((stages, 2, pair, hs), F32),
@@ -342,6 +372,16 @@
         ),
         name="attention_backward",
     )(queries, keys, values, grad_out, out_weight, segments.reshape(1, rows))
+    anywhere = pl.BlockSpec(memory_space=pl.ANY)
+    return pl.pallas_call(
+        hand_over,
+        out_shape=tuple(jax.ShapeDtypeStruct(a.shape, a.dtype) for a in grads),
+        in_specs=[anywhere] * 3,
+        out_specs=(anywhere,) * 3,
+        scratch_shapes=[dma((3,))],
+        compiler_params=pltpu.CompilerParams(vmem_limit_bytes=56 * 1024 * 1024),
+        name="hand_over",
+    )(*grads)
 
 
 def solution(mesh):

time: 45.5 us -> 53.7 us (1.18)
  Pallas kernels: 40 us -> 52.9 us
  local copies, waits for them, and re-layouts: 4.61 us -> 0 us
    pallas_call x0 -> x1, Pallas kernels: none -> 13 us  [per_device(): pl.pallas_call(hand_over, out_shape=tuple((jax.ShapeDtypeStruct(a.shape,...]
    unnamed x3 -> x0, local copies, waits for them, and re-layouts: 4.61 us -> none
where the time goes in v2:
time: 53.7 us; the launch traced here: 53.5 us
  Pallas kernels  52.9 us (99%)
  between operations  0.64 us (1%)
    pallas_call x1, Pallas kernels, per_device(): pl.pallas_call(functools.partial(kernel, stages), out_shape=(jax.ShapeDty...  39.9 us
    pallas_call x1, Pallas kernels, per_device(): pl.pallas_call(hand_over, out_shape=tuple((jax.ShapeDtypeStruct(a.shape,...  13 us

profile of v2, /device:TPU:0, one launch (start us, length us, event | category | flops | bytes accessed | tf_op | source)
XLA Modules:
  0.0 53.5 jit_solution(7065659631527521308)
XLA Ops:
  0.6 39.9 %attention_backward.1 = (bf16[128,1024]{1,0:T(8,128)(2,1)}, bf16[128,256]{1,0:T(8,128)(2,1)}, bf16[128,256]{1,0:T(8,128)(2,1)}) custom-call(bf16[128,1024]{1,0:T(8,128)(2,1)} %q_in.1, bf16[128,256]{1,0:T(8,128)(2,1)} %k_in.1, bf16[128,256]{1,0:T(8,128)(2,1)} %v_in.1, bf16[128,1024]{1,0:T(8,128)(2,1)} %g_in.1, bf16[4096,1024]{1,0:T(8,128)(2,1)} %w_hbm.1, ...), custom_call_target="tpu_custom_call" | custom-call | tf_op jit(solution)/shard_map/attention_backward/pallas_call | solution.py:333
  40.5 13.0 %hand_over.1 = (bf16[128,1024]{1,0:T(8,128)(2,1)}, bf16[128,256]{1,0:T(8,128)(2,1)}, bf16[128,256]{1,0:T(8,128)(2,1)}) custom-call(bf16[128,1024]{1,0:T(8,128)(2,1)} %get-tuple-element.6.a, bf16[128,256]{1,0:T(8,128)(2,1)} %get-tuple-element.7.b, bf16[128,256]{1,0:T(8,128)(2,1)} %get-tuple-element.8.c), custom_call_target="tpu_custom_call" | custom-call | tf_op jit(solution)/shard_map/hand_over/pallas_call | solution.py:376

commit v3 on v2

--- a/solution.py
+++ b/solution.py
@@ -27,8 +27,8 @@
     stages, q_in, k_in, v_in, g_in, w_hbm, seg_in,
     q_out, k_out, v_out,
     wbuf, gbuf, acc, kv, ky, qbuf, ubuf, usend, mst, lst, wst, ones, ot, kept,
-    dq, dqs, dqr, own, rs, ret, fins, finr,
-    w_sem, gx_s, gx_r, gc_s, gc_r, gf_s, gf_r, kv_s, kv_r, ret_s, ret_r,
+    dq, dqs, dqr, own, rs, ret, retd, fins, finr,
+    w_sem, gx_s, gx_r, gc_s, gc_r, gf_s, gf_r, kv_s, kv_r, ret_s, ret_r, dia_s, dia_r,
     misc_s, misc_r, fin_s, fin_r,
 ):
     rows = k_in.shape[0]
@@ -46,12 +46,14 @@
     sib = (2 * s + z, tp)
     down = (2 * lax.rem(s + 1, stages) + y, tp)
     up = (2 * lax.rem(s + stages - 1, stages) + y, tp)
+    down_d = (2 * lax.rem(s + 1, stages) + z, tp)
+    up_d = (2 * lax.rem(s + stages - 1, stages) + z, tp)
     xnb = (ctx, 2 * (1 - x) + c)
     core = (ctx, 2 * x + 1 - c)
     t_own, t_core, t_x, t_f = tp, 2 * x + 1 - c, 2 * (1 - x) + c, 2 * (1 - x) + 1 - c
 
     barrier = pltpu.get_barrier_semaphore()
-    for dev in (sib, down, up, xnb, core):
+    for dev in (sib, down, up, down_d, up_d, xnb, core):
         pl.semaphore_signal(barrier, inc=1, device_id=dev, device_id_type=MESH)
 
     def remote(src, dst, a, b, dev):
@@ -76,7 +78,7 @@
     fill(kv.at[s, y], y)
     fill(ky, z)
 
-    pl.semaphore_wait(barrier, 5)
+    pl.semaphore_wait(barrier, 7)
 
     def chain(k, p):
         return remote(kv.at[k, p], kv.at[k, p], kv_s.at[k, p], kv_r.at[k, p], down)
@@ -105,10 +107,8 @@
     def _():
         chain(s, y).start()
 
-    gx[1].start()
     gc[0].start()
     gc[1].start()
-    q_copy.start()
 
     qbuf[y] = q_in[:, pl.ds(pl.multiple_of(y * gw, gw), gw)]
 
@@ -120,6 +120,7 @@
     acc[...] += product(g_in[:, half:], t_own, 1)
 
     ky_copy.wait_recv()
+    q_copy.start()
 
     @pl.when(jnp.logical_not(last))
     def _():
@@ -128,6 +129,8 @@
     for h in range(2):
         gc[h].wait_recv()
         acc[...] += product(gbuf[t_core, h], t_core, h)
+    gx[0].wait_send()
+    gx[1].start()
     gx[0].wait_recv()
     gf[0].start()
 
@@ -226,8 +229,24 @@
     mst[...] = mst[...] + jnp.log2(lst[...])
     wst[...] = wst[...] / lst[...]
 
+    here = pl.ds(pl.multiple_of(y * rows, rows), rows)
+    there = pl.ds(pl.multiple_of(z * rows, rows), rows)
+
     def back(k, p):
         return remote(rs.at[k, p], ret.at[k, p], ret_s.at[k, p], ret_r.at[k, p], up)
+
+    def home(p):
+        k = s - 1
+        return (
+            remote(rs.at[k, p, here], ret.at[k, p, here], ret_s.at[k, p], ret_r.at[k, p], up),
+            remote(rs.at[k, p, there], retd.at[p], dia_s.at[p], dia_r.at[p], up_d),
+        )
+
+    def home_arrived(p):
+        remote(rs.at[s, p, here], ret.at[s, p, here], ret_s.at[s, p], ret_r.at[s, p], up).wait_recv()
+        remote(rs.at[s, p, there], retd.at[p], dia_s.at[p], dia_r.at[p], up_d).wait_recv()
+
+    fin = [remote(fins.at[p], finr.at[p], fin_s.at[p], fin_r.at[p], sib) for p in range(2)]
 
     def gradients(k, carry):
         if keep:
@@ -252,6 +271,15 @@
         def _():
             for p in range(2):
                 rs[k, p] = own[k, p].astype(BF16)
+
+        @pl.when(last & (k >= 1) & (k < s))
+        def _():
+            for p in range(2):
+                back(k - 1, p).wait_send()
+
+        @pl.when(last & (k < s - 1))
+        def _():
+            for p in range(2):
                 back(k, p).start()
 
         return carry
@@ -268,35 +296,55 @@
             dq[r, :, pl.ds(pl.multiple_of(y * rows, rows), rows)] * scale
         ).T.astype(BF16)
 
+    for p in range(2):
+        fins[p] = own[s, p, there, :]
+        fin[p].start()
+
+    @pl.when(last & (s >= 1))
+    def _():
+        for p in range(2):
+            for copy in home(p):
+                copy.start()
+
     @pl.when(jnp.logical_not(last))
     def _():
         def body(k, carry):
             for p in range(2):
                 back(k, p).wait_recv()
                 rs[k, p] = (own[k, p] + ret[k, p].astype(F32)).astype(BF16)
-                back(k, p).start()
+
+                @pl.when(k < s - 1)
+                def _():
+                    back(k, p).start()
+
+                @pl.when(k == s - 1)
+                def _():
+                    for copy in home(p):
+                        copy.start()
+
             return carry
 
         lax.fori_loop(0, s, body, 0)
-        for p in range(2):
-            back(s, p).wait_recv()
-            own[s, p] = own[s, p] + ret[s, p].astype(F32)
-
-    fin = [remote(fins.at[p], finr.at[p], fin_s.at[p], fin_r.at[p], sib) for p in range(2)]
-    for p in range(2):
-        fins[p] = own[s, p, pl.ds(pl.multiple_of(z * rows, rows), rows), :].astype(BF16)
-        fin[p].start()
+
+    dq_copy.wait_recv()
+    q_out[:, pl.ds(pl.multiple_of(z * gw, gw), gw)] = dqr[...]
     mine = pl.ds(pl.multiple_of(y * hs, hs), hs)
     theirs = pl.ds(pl.multiple_of(z * hs, hs), hs)
     for p, out in enumerate((k_out, v_out)):
-        out[:, mine] = own[s, p, pl.ds(pl.multiple_of(y * rows, rows), rows), :].astype(BF16)
-    dq_copy.wait_recv()
-    q_out[:, pl.ds(pl.multiple_of(z * gw, gw), gw)] = dqr[...]
-    for p, out in enumerate((k_out, v_out)):
         fin[p].wait_recv()
-        out[:, theirs] = finr[p]
-
-    for copy in (ky_copy, q_copy, u_copy, dq_copy, *gx, *gc, *gf, *fin):
+
+        @pl.when(last)
+        def _():
+            out[:, mine] = own[s, p, here, :].astype(BF16)
+            out[:, theirs] = finr[p].astype(BF16)
+
+        @pl.when(jnp.logical_not(last))
+        def _():
+            home_arrived(p)
+            out[:, mine] = (own[s, p, here, :] + ret[s, p, here, :].astype(F32)).astype(BF16)
+            out[:, theirs] = (finr[p] + retd[p].astype(F32)).astype(BF16)
+
+    for copy in (ky_copy, q_copy, u_copy, dq_copy, gx[1], *gc, *gf, *fin):
         copy.wait_send()
 
     @pl.when(jnp.logical_not(last))
@@ -308,20 +356,26 @@
 
         lax.fori_loop(0, s + 1, body, 0)
 
-    def drain(k, carry):
+    @pl.when(jnp.logical_not(last))
+    def _():
+        def body(k, carry):
+            for p in range(2):
+                back(k, p).wait_send()
+            return carry
+
+        lax.fori_loop(0, s - 1, body, 0)
+
+    @pl.when(s >= 1)
+    def _():
         for p in range(2):
-            back(k, p).wait_send()
-        return carry
-
-    lax.fori_loop(0, s, drain, 0)
-
-
-def hand_over(a, b, c, x, y, z, sem):
-    copies = [pltpu.make_async_copy(p, q, sem.at[i]) for i, (p, q) in enumerate(((a, x), (b, y), (c, z)))]
-    for copy in copies:
-        copy.start()
-    for copy in copies:
-        copy.wait()
+            for copy in home(p):
+                copy.wait_send()
+
+
+def hand_over(a, b, c, x, y, z):
+    x[...] = a[...]
+    y[...] = b[...]
+    z[...] = c[...]
 
 
 def per_device(stages, queries, keys, values, grad_out, out_weight, segments):
@@ -361,10 +415,11 @@
             pltpu.VMEM((stages, 2, pair, hs), BF16),
             pltpu.VMEM((stages, 2, pair, hs), BF16),
             pltpu.VMEM((2, rows, hs), BF16),
-            pltpu.VMEM((2, rows, hs), BF16),
+            pltpu.VMEM((2, rows, hs), F32),
+            pltpu.VMEM((2, rows, hs), F32),
             dma((8,)),
             dma((2,)), dma((2,)), dma((2,)), dma((2,)), dma((2,)), dma((2,)),
-            dma((stages, 2)), dma((stages, 2)), dma((stages, 2)), dma((stages, 2)),
+            dma((stages, 2)), dma((stages, 2)), dma((stages, 2)), dma((stages, 2)), dma((2,)), dma((2,)),
             dma((4,)), dma((4,)), dma((2,)), dma((2,)),
         ],
         compiler_params=pltpu.CompilerParams(
@@ -372,13 +427,11 @@
         ),
         name="attention_backward",
     )(queries, keys, values, grad_out, out_weight, segments.reshape(1, rows))
-    anywhere = pl.BlockSpec(memory_space=pl.ANY)
     return pl.pallas_call(
         hand_over,
         out_shape=tuple(jax.ShapeDtypeStruct(a.shape, a.dtype) for a in grads),
-        in_specs=[anywhere] * 3,
-        out_specs=(anywhere,) * 3,
-        scratch_shapes=[dma((3,))],
+        in_specs=[vmem] * 3,
+        out_specs=(vmem,) * 3,
         compiler_params=pltpu.CompilerParams(vmem_limit_bytes=56 * 1024 * 1024),
         name="hand_over",
     )(*grads)

time: 53.7 us -> 39.8 us (0.74)
  Pallas kernels: 52.9 us -> 39 us
    pallas_call x1, Pallas kernels: 13 us -> 1.73 us  [per_device(): pl.pallas_call(hand_over, out_shape=tuple((jax.ShapeDtypeStruct(a.shape,...]
    pallas_call x1, Pallas kernels: 39.9 us -> 37.2 us  [per_device(): pl.pallas_call(functools.partial(kernel, stages), out_shape=(jax.ShapeDty...]
where the time goes in v3:
time: 39.8 us; the launch traced here: 39.6 us
  Pallas kernels  39 us (98%)
  between operations  0.64 us (2%)
    pallas_call x1, Pallas kernels, per_device(): pl.pallas_call(functools.partial(kernel, stages), out_shape=(jax.ShapeDty...  37.2 us
    pallas_call x1, Pallas kernels, per_device(): pl.pallas_call(hand_over, out_shape=tuple((jax.ShapeDtypeStruct(a.shape,...  1.73 us

profile of v3, /device:TPU:0, one launch (start us, length us, event | category | flops | bytes accessed | tf_op | source)
XLA Modules:
  0.0 39.6 jit_solution(297382187368061459)
XLA Ops:
  0.6 37.2 %attention_backward.1 = (bf16[128,1024]{1,0:T(8,128)(2,1)}, bf16[128,256]{1,0:T(8,128)(2,1)}, bf16[128,256]{1,0:T(8,128)(2,1)}) custom-call(bf16[128,1024]{1,0:T(8,128)(2,1)} %q_in.1, bf16[128,256]{1,0:T(8,128)(2,1)} %k_in.1, bf16[128,256]{1,0:T(8,128)(2,1)} %v_in.1, bf16[128,1024]{1,0:T(8,128)(2,1)} %g_in.1, bf16[4096,1024]{1,0:T(8,128)(2,1)} %w_hbm.1, ...), custom_call_target="tpu_custom_call" | custom-call | tf_op jit(solution)/shard_map/attention_backward/pallas_call | solution.py:387
  37.9 1.7 %hand_over.1 = (bf16[128,1024]{1,0:T(8,128)(2,1)}, bf16[128,256]{1,0:T(8,128)(2,1)}, bf16[128,256]{1,0:T(8,128)(2,1)}) custom-call(bf16[128,1024]{1,0:T(8,128)(2,1)} %get-tuple-element.6.a, bf16[128,256]{1,0:T(8,128)(2,1)} %get-tuple-element.7.b, bf16[128,256]{1,0:T(8,128)(2,1)} %get-tuple-element.8.c), custom_call_target="tpu_custom_call" | custom-call | tf_op jit(solution)/shard_map/hand_over/pallas_call | solution.py:430

commit v4 on v3

--- a/solution.py
+++ b/solution.py
@@ -13,6 +13,7 @@
 RATIO = QUERY_HEADS // KEY_VALUE_HEADS
 SEG_ROWS = 16
 KEPT_STAGES = 8
+PARTS = 4
 LOG2E = 1.4426950408889634
 MESH = pl.DeviceIdType.MESH
 F32 = jnp.float32
@@ -24,19 +25,19 @@
 
 
 def kernel(
-    stages, q_in, k_in, v_in, g_in, w_hbm, seg_in,
+    stages, q_in, k_hbm, v_hbm, g_in, w_hbm, seg_hbm,
     q_out, k_out, v_out,
-    wbuf, gbuf, acc, kv, ky, qbuf, ubuf, usend, mst, lst, wst, ones, ot, kept,
+    k_in, v_in, seg_in, wbuf, gbuf, acc, kv, ky, qbuf, ubuf, usend, mst, lst, wst, ones, ot, kept,
     dq, dqs, dqr, own, rs, ret, retd, fins, finr,
-    w_sem, gx_s, gx_r, gc_s, gc_r, gf_s, gf_r, kv_s, kv_r, ret_s, ret_r, dia_s, dia_r,
+    w_sem, in_sem, gx_s, gx_r, gc_s, gc_r, gf_s, gf_r, kv_s, kv_r, ret_s, ret_r, dia_s, dia_r,
     misc_s, misc_r, fin_s, fin_r,
 ):
-    rows = k_in.shape[0]
+    rows = k_hbm.shape[0]
     pair = 2 * rows
     hs = HEAD_SIZE
     gw = RATIO * hs
     keep = stages <= KEPT_STAGES
-    half = g_in.shape[1] // 2
+    part = g_in.shape[1] // PARTS
     scale = HEAD_SIZE ** -0.5
     ctx = lax.axis_index("ctx")
     tp = lax.axis_index("tp")
@@ -62,12 +63,27 @@
         )
 
     def w_copy(t, h):
-        i = 2 * t + h
-        return pltpu.make_async_copy(w_hbm.at[pl.ds(i * half, half)], wbuf.at[i], w_sem.at[i])
-
+        i = PARTS * t + h
+        return pltpu.make_async_copy(w_hbm.at[pl.ds(i * part, part)], wbuf.at[i], w_sem.at[i])
+
+    def g_part(h):
+        return g_in.at[:, h * part : (h + 1) * part]
+
+    own_q = pl.ds(pl.multiple_of(y * gw, gw), gw)
+    loads = [
+        pltpu.make_async_copy(src, dst, in_sem.at[i])
+        for i, (src, dst) in enumerate(
+            [(k_hbm, k_in), (v_hbm, v_in), (seg_hbm, seg_in), (q_in.at[:, own_q], qbuf.at[y])]
+            + [(g_part(h), gbuf.at[t_own, h]) for h in range(PARTS)]
+        )
+    ]
+    for copy in loads:
+        copy.start()
     for t in (t_own, t_core, t_x, t_f):
-        for h in range(2):
+        for h in range(PARTS):
             w_copy(t, h).start()
+    for copy in loads[:3]:
+        copy.wait()
 
     def fill(dst, g):
         cols = pl.ds(pl.multiple_of(g * hs, hs), hs)
@@ -89,35 +105,32 @@
     )
     u_copy = remote(usend, ubuf.at[y], misc_s.at[2], misc_r.at[2], sib)
     dq_copy = remote(dqs, dqr, misc_s.at[3], misc_r.at[3], sib)
-    gx = [
-        remote(g_in.at[:, h * half : (h + 1) * half], gbuf.at[t_own, h], gx_s.at[h], gx_r.at[h], xnb)
-        for h in range(2)
-    ]
-    gc = [
-        remote(g_in.at[:, h * half : (h + 1) * half], gbuf.at[t_own, h], gc_s.at[h], gc_r.at[h], core)
-        for h in range(2)
-    ]
-    gf = [remote(gbuf.at[t_x, h], gbuf.at[t_x, h], gf_s.at[h], gf_r.at[h], core) for h in range(2)]
+    parts = range(PARTS)
+    gx = [remote(g_part(h), gbuf.at[t_own, h], gx_s.at[h], gx_r.at[h], xnb) for h in parts]
+    gc = [remote(g_part(h), gbuf.at[t_own, h], gc_s.at[h], gc_r.at[h], core) for h in parts]
+    gf = [remote(gbuf.at[t_x, h], gbuf.at[t_x, h], gf_s.at[h], gf_r.at[h], core) for h in parts]
     last = s == stages - 1
 
     ky_copy.start()
     gx[0].start()
+    gx[1].start()
 
     @pl.when(jnp.logical_not(last))
     def _():
         chain(s, y).start()
 
-    gc[0].start()
-    gc[1].start()
-
-    qbuf[y] = q_in[:, pl.ds(pl.multiple_of(y * gw, gw), gw)]
-
-    def product(left, t, h):
+    for copy in gc:
+        copy.start()
+
+    def product(t, h):
         w_copy(t, h).wait()
-        return dot(left, wbuf[2 * t + h], 1, 0)
-
-    acc[...] = product(g_in[:, 0:half], t_own, 0)
-    acc[...] += product(g_in[:, half:], t_own, 1)
+        return dot(gbuf[t, h], wbuf[PARTS * t + h], 1, 0)
+
+    for copy in loads[3:]:
+        copy.wait()
+    acc[...] = product(t_own, 0)
+    for h in range(1, PARTS):
+        acc[...] += product(t_own, h)
 
     ky_copy.wait_recv()
     q_copy.start()
@@ -126,13 +139,13 @@
     def _():
         chain(s, z).start()
 
-    for h in range(2):
+    gx[0].wait_send()
+    gx[2].start()
+    for h in parts:
         gc[h].wait_recv()
-        acc[...] += product(gbuf[t_core, h], t_core, h)
-    gx[0].wait_send()
-    gx[1].start()
-    gx[0].wait_recv()
-    gf[0].start()
+        acc[...] += product(t_core, h)
+    gx[1].wait_send()
+    gx[3].start()
 
     def arrive(k):
         for p in range(2):
@@ -142,22 +155,23 @@
             def _():
                 chain(k, p).start()
 
-    @pl.when(s >= 1)
-    def _():
-        arrive(s - 1)
-
-    acc[...] += product(gbuf[t_x, 0], t_x, 0)
-    gx[1].wait_recv()
-    gf[1].start()
-
-    @pl.when((s >= 2) & jnp.logical_not(last))
-    def _():
-        arrive(s - 2)
-
-    acc[...] += product(gbuf[t_x, 1], t_x, 1)
-    for h in range(2):
+    for h in parts:
+        gx[h].wait_recv()
+        gf[h].start()
+        if h == 0:
+            @pl.when(s >= 1)
+            def _():
+                arrive(s - 1)
+
+        if h == PARTS - 1:
+            @pl.when((s >= 2) & jnp.logical_not(last))
+            def _():
+                arrive(s - 2)
+
+        acc[...] += product(t_x, h)
+    for h in parts:
         gf[h].wait_recv()
-        acc[...] += product(gbuf[t_f, h], t_f, h)
+        acc[...] += product(t_f, h)
     usend[...] = acc[:, pl.ds(pl.multiple_of(z * gw, gw), gw)].astype(BF16)
     u_copy.start()
     ubuf[y] = acc[:, pl.ds(pl.multiple_of(y * gw, gw), gw)].astype(BF16)
@@ -272,14 +286,13 @@
             for p in range(2):
                 rs[k, p] = own[k, p].astype(BF16)
 
-        @pl.when(last & (k >= 1) & (k < s))
-        def _():
-            for p in range(2):
-                back(k - 1, p).wait_send()
-
         @pl.when(last & (k < s - 1))
         def _():
             for p in range(2):
+                @pl.when(k >= 1)
+                def _():
+                    back(k - 1, p).wait_send()
+
                 back(k, p).start()
 
         return carry
@@ -303,6 +316,10 @@
     @pl.when(last & (s >= 1))
     def _():
         for p in range(2):
+            @pl.when(s >= 2)
+            def _():
+                back(s - 2, p).wait_send()
+
             for copy in home(p):
                 copy.start()
 
@@ -344,7 +361,7 @@
             out[:, mine] = (own[s, p, here, :] + ret[s, p, here, :].astype(F32)).astype(BF16)
             out[:, theirs] = (finr[p] + retd[p].astype(F32)).astype(BF16)
 
-    for copy in (ky_copy, q_copy, u_copy, dq_copy, gx[1], *gc, *gf, *fin):
+    for copy in (ky_copy, q_copy, u_copy, dq_copy, gx[2], gx[3], *gc, *gf, *fin):
         copy.wait_send()
 
     @pl.when(jnp.logical_not(last))
@@ -391,11 +408,14 @@
             jax.ShapeDtypeStruct(keys.shape, BF16),
             jax.ShapeDtypeStruct(values.shape, BF16),
         ),
-        in_specs=[vmem, vmem, vmem, vmem, pl.BlockSpec(memory_space=pl.ANY), vmem],
+        in_specs=[pl.BlockSpec(memory_space=pl.ANY)] * 6,
         out_specs=(vmem, vmem, vmem),
         scratch_shapes=[
-            pltpu.VMEM((8, depth // 2, wide), BF16),
-            pltpu.VMEM((4, 2, rows, depth // 2), BF16),
+            pltpu.VMEM(keys.shape, BF16),
+            pltpu.VMEM(values.shape, BF16),
+            pltpu.VMEM((1, rows), jnp.int32),
+            pltpu.VMEM((4 * PARTS, depth // PARTS, wide), BF16),
+            pltpu.VMEM((4, PARTS, rows, depth // PARTS), BF16),
             pltpu.VMEM((rows, wide), F32),
             pltpu.VMEM((stages, 2, pair + SEG_ROWS, hs), BF16),
             pltpu.VMEM((pair + SEG_ROWS, hs), BF16),
@@ -417,8 +437,8 @@
             pltpu.VMEM((2, rows, hs), BF16),
             pltpu.VMEM((2, rows, hs), F32),
             pltpu.VMEM((2, rows, hs), F32),
-            dma((8,)),
-            dma((2,)), dma((2,)), dma((2,)), dma((2,)), dma((2,)), dma((2,)),
+            dma((4 * PARTS,)), dma((4 + PARTS,)),
+            *[dma((PARTS,))] * 6,
             dma((stages, 2)), dma((stages, 2)), dma((stages, 2)), dma((stages, 2)), dma((2,)), dma((2,)),
             dma((4,)), dma((4,)), dma((2,)), dma((2,)),
         ],

time: 39.8 us -> 39.7 us (level)
  no operation moved by 1% of the time
where the time goes in v4:
time: 39.7 us; the launch traced here: 39.5 us
  Pallas kernels  38.9 us (98%)
  between operations  0.64 us (2%)
    pallas_call x1, Pallas kernels, per_device(): pl.pallas_call(functools.partial(kernel, stages), out_shape=(jax.ShapeDty...  37.1 us
    pallas_call x1, Pallas kernels, per_device(): pl.pallas_call(hand_over, out_shape=tuple((jax.ShapeDtypeStruct(a.shape,...  1.73 us

profile of v4, /device:TPU:0, one launch (start us, length us, event | category | flops | bytes accessed | tf_op | source)
XLA Modules:
  0.0 39.5 jit_solution(1841191880572253740)
XLA Ops:
  0.6 37.1 %attention_backward.1 = (bf16[128,1024]{1,0:T(8,128)(2,1)}, bf16[128,256]{1,0:T(8,128)(2,1)}, bf16[128,256]{1,0:T(8,128)(2,1)}) custom-call(bf16[128,1024]{1,0:T(8,128)(2,1)} %q_in.1, bf16[128,256]{1,0:T(8,128)(2,1)} %k_hbm.1, bf16[128,256]{1,0:T(8,128)(2,1)} %v_hbm.1, bf16[128,1024]{1,0:T(8,128)(2,1)} %g_in.1, bf16[4096,1024]{1,0:T(8,128)(2,1)} %w_hbm.1, ...), custom_call_target="tpu_custom_call" | custom-call | tf_op jit(solution)/shard_map/attention_backward/pallas_call | solution.py:404
  37.8 1.7 %hand_over.1 = (bf16[128,1024]{1,0:T(8,128)(2,1)}, bf16[128,256]{1,0:T(8,128)(2,1)}, bf16[128,256]{1,0:T(8,128)(2,1)}) custom-call(bf16[128,1024]{1,0:T(8,128)(2,1)} %get-tuple-element.6.a, bf16[128,256]{1,0:T(8,128)(2,1)} %get-tuple-element.7.b, bf16[128,256]{1,0:T(8,128)(2,1)} %get-tuple-element.8.c), custom_call_target="tpu_custom_call" | custom-call | tf_op jit(solution)/shard_map/hand_over/pallas_call | solution.py:450

commit v5 on v4

--- a/solution.py
+++ b/solution.py
@@ -112,8 +112,8 @@
     last = s == stages - 1
 
     ky_copy.start()
-    gx[0].start()
-    gx[1].start()
+    for copy in gx:
+        copy.start()
 
     @pl.when(jnp.logical_not(last))
     def _():
@@ -139,29 +139,28 @@
     def _():
         chain(s, z).start()
 
-    gx[0].wait_send()
-    gx[2].start()
     for h in parts:
         gc[h].wait_recv()
         acc[...] += product(t_core, h)
-    gx[1].wait_send()
-    gx[3].start()
+
+    def arrive_part(k, p):
+        chain(k, p).wait_recv()
+
+        @pl.when(jnp.logical_not(last))
+        def _():
+            chain(k, p).start()
 
     def arrive(k):
         for p in range(2):
-            chain(k, p).wait_recv()
-
-            @pl.when(jnp.logical_not(last))
-            def _():
-                chain(k, p).start()
+            arrive_part(k, p)
 
     for h in parts:
         gx[h].wait_recv()
         gf[h].start()
-        if h == 0:
+        if h in (0, 2):
             @pl.when(s >= 1)
             def _():
-                arrive(s - 1)
+                arrive_part(s - 1, z if h else y)
 
         if h == PARTS - 1:
             @pl.when((s >= 2) & jnp.logical_not(last))
@@ -169,22 +168,6 @@
                 arrive(s - 2)
 
         acc[...] += product(t_x, h)
-    for h in parts:
-        gf[h].wait_recv()
-        acc[...] += product(t_f, h)
-    usend[...] = acc[:, pl.ds(pl.multiple_of(z * gw, gw), gw)].astype(BF16)
-    u_copy.start()
-    ubuf[y] = acc[:, pl.ds(pl.multiple_of(y * gw, gw), gw)].astype(BF16)
-
-    @pl.when(jnp.logical_not(last))
-    def _():
-        def body(i, carry):
-            arrive(s - 3 - i)
-            return carry
-
-        lax.fori_loop(0, s - 2, body, 0)
-
-    q_copy.wait_recv()
 
     mst[...] = jnp.full(mst.shape, -1e20, F32)
     lst[...] = jnp.zeros(lst.shape, F32)
@@ -236,7 +219,25 @@
             ot[r] = ot[r] * factor + dot(turned, pr.astype(BF16), 1, 0)
         return carry
 
-    lax.fori_loop(0, s + 1, statistics, 0)
+    for h in parts:
+        if h == PARTS - 1:
+            q_copy.wait_recv()
+            statistics(0, 0)
+        gf[h].wait_recv()
+        acc[...] += product(t_f, h)
+    usend[...] = acc[:, pl.ds(pl.multiple_of(z * gw, gw), gw)].astype(BF16)
+    u_copy.start()
+    ubuf[y] = acc[:, pl.ds(pl.multiple_of(y * gw, gw), gw)].astype(BF16)
+
+    @pl.when(jnp.logical_not(last))
+    def _():
+        def body(i, carry):
+            arrive(s - 3 - i)
+            return carry
+
+        lax.fori_loop(0, s - 2, body, 0)
+
+    lax.fori_loop(1, s + 1, statistics, 0)
     u_copy.wait_recv()
     for r in range(RATIO):
         wst[r : r + 1, :] = jnp.sum(heads(ubuf, r).astype(F32).T * ot[r], axis=0, keepdims=True)
@@ -289,11 +290,13 @@
         @pl.when(last & (k < s - 1))
         def _():
             for p in range(2):
-                @pl.when(k >= 1)
-                def _():
-                    back(k - 1, p).wait_send()
-
                 back(k, p).start()
+
+        @pl.when(last & (k == s - 1))
+        def _():
+            for p in range(2):
+                for copy in home(p):
+                    copy.start()
 
         return carry
 
@@ -313,16 +316,6 @@
         fins[p] = own[s, p, there, :]
         fin[p].start()
 
-    @pl.when(last & (s >= 1))
-    def _():
-        for p in range(2):
-            @pl.when(s >= 2)
-            def _():
-                back(s - 2, p).wait_send()
-
-            for copy in home(p):
-                copy.start()
-
     @pl.when(jnp.logical_not(last))
     def _():
         def body(k, carry):
@@ -361,7 +354,7 @@
             out[:, mine] = (own[s, p, here, :] + ret[s, p, here, :].astype(F32)).astype(BF16)
             out[:, theirs] = (finr[p] + retd[p].astype(F32)).astype(BF16)
 
-    for copy in (ky_copy, q_copy, u_copy, dq_copy, gx[2], gx[3], *gc, *gf, *fin):
+    for copy in (ky_copy, q_copy, u_copy, dq_copy, *gx, *gc, *gf, *fin):
         copy.wait_send()
 
     @pl.when(jnp.logical_not(last))
@@ -373,14 +366,12 @@
 
         lax.fori_loop(0, s + 1, body, 0)
 
-    @pl.when(jnp.logical_not(last))
-    def _():
-        def body(k, carry):
-            for p in range(2):
-                back(k, p).wait_send()
-            return carry
-
-        lax.fori_loop(0, s - 1, body, 0)
+    def drain(k, carry):
+        for p in range(2):
+            back(k, p).wait_send()
+        return carry
+
+    lax.fori_loop(0, s - 1, drain, 0)
 
     @pl.when(s >= 1)
     def _():

time: 39.7 us -> 39.1 us (0.985)
  Pallas kernels: 38.9 us -> 38.3 us
    pallas_call x1, Pallas kernels: 37.1 us -> 36.5 us  [per_device(): pl.pallas_call(functools.partial(kernel, stages), out_shape=(jax.ShapeDty...]
where the time goes in v5:
time: 39.1 us; the launch traced here: 38.9 us
  Pallas kernels  38.3 us (98%)
  between operations  0.64 us (2%)
    pallas_call x1, Pallas kernels, per_device(): pl.pallas_call(functools.partial(kernel, stages), out_shape=(jax.ShapeDty...  36.5 us
    pallas_call x1, Pallas kernels, per_device(): pl.pallas_call(hand_over, out_shape=tuple((jax.ShapeDtypeStruct(a.shape,...  1.73 us

profile of v5, /device:TPU:0, one launch (start us, length us, event | category | flops | bytes accessed | tf_op | source)
XLA Modules:
  0.0 38.9 jit_solution(1870773808785881127)
XLA Ops:
  0.6 36.5 %attention_backward.1 = (bf16[128,1024]{1,0:T(8,128)(2,1)}, bf16[128,256]{1,0:T(8,128)(2,1)}, bf16[128,256]{1,0:T(8,128)(2,1)}) custom-call(bf16[128,1024]{1,0:T(8,128)(2,1)} %q_in.1, bf16[128,256]{1,0:T(8,128)(2,1)} %k_hbm.1, bf16[128,256]{1,0:T(8,128)(2,1)} %v_hbm.1, bf16[128,1024]{1,0:T(8,128)(2,1)} %g_in.1, bf16[4096,1024]{1,0:T(8,128)(2,1)} %w_hbm.1, ...), custom_call_target="tpu_custom_call" | custom-call | tf_op jit(solution)/shard_map/attention_backward/pallas_call | solution.py:395
  37.2 1.7 %hand_over.1 = (bf16[128,1024]{1,0:T(8,128)(2,1)}, bf16[128,256]{1,0:T(8,128)(2,1)}, bf16[128,256]{1,0:T(8,128)(2,1)}) custom-call(bf16[128,1024]{1,0:T(8,128)(2,1)} %get-tuple-element.6.a, bf16[128,256]{1,0:T(8,128)(2,1)} %get-tuple-element.7.b, bf16[128,256]{1,0:T(8,128)(2,1)} %get-tuple-element.8.c), custom_call_target="tpu_custom_call" | custom-call | tf_op jit(solution)/shard_map/hand_over/pallas_call | solution.py:441

commit v6 on v5

--- a/solution.py
+++ b/solution.py
@@ -247,19 +247,22 @@
     here = pl.ds(pl.multiple_of(y * rows, rows), rows)
     there = pl.ds(pl.multiple_of(z * rows, rows), rows)
 
-    def back(k, p):
-        return remote(rs.at[k, p], ret.at[k, p], ret_s.at[k, p], ret_r.at[k, p], up)
-
-    def home(p):
-        k = s - 1
-        return (
-            remote(rs.at[k, p, here], ret.at[k, p, here], ret_s.at[k, p], ret_r.at[k, p], up),
-            remote(rs.at[k, p, there], retd.at[p], dia_s.at[p], dia_r.at[p], up_d),
+    halves = (here, there)
+
+    def back(k, p, h):
+        return remote(
+            rs.at[k, p, halves[h]], ret.at[k, p, halves[h]],
+            ret_s.at[k, 2 * p + h], ret_r.at[k, 2 * p + h], up,
         )
 
-    def home_arrived(p):
-        remote(rs.at[s, p, here], ret.at[s, p, here], ret_s.at[s, p], ret_r.at[s, p], up).wait_recv()
-        remote(rs.at[s, p, there], retd.at[p], dia_s.at[p], dia_r.at[p], up_d).wait_recv()
+    def home(k, p, h):
+        if h == 0:
+            return remote(
+                rs.at[k, p, here], ret.at[k, p, here], ret_s.at[k, 2 * p], ret_r.at[k, 2 * p], up
+            )
+        return remote(rs.at[k, p, there], retd.at[p], dia_s.at[p], dia_r.at[p], up_d)
+
+    pieces4 = [(p, h) for p in range(2) for h in range(2)]
 
     fin = [remote(fins.at[p], finr.at[p], fin_s.at[p], fin_r.at[p], sib) for p in range(2)]
 
@@ -287,16 +290,20 @@
             for p in range(2):
                 rs[k, p] = own[k, p].astype(BF16)
 
+        @pl.when(last & (k >= 2) & (k < s))
+        def _():
+            for p, h in pieces4:
+                back(k - 2, p, h).wait_send()
+
         @pl.when(last & (k < s - 1))
         def _():
-            for p in range(2):
-                back(k, p).start()
+            for p, h in pieces4:
+                back(k, p, h).start()
 
         @pl.when(last & (k == s - 1))
         def _():
-            for p in range(2):
-                for copy in home(p):
-                    copy.start()
+            for p, h in pieces4:
+                home(s - 1, p, h).start()
 
         return carry
 
@@ -320,17 +327,19 @@
     def _():
         def body(k, carry):
             for p in range(2):
-                back(k, p).wait_recv()
-                rs[k, p] = (own[k, p] + ret[k, p].astype(F32)).astype(BF16)
-
-                @pl.when(k < s - 1)
-                def _():
-                    back(k, p).start()
-
-                @pl.when(k == s - 1)
-                def _():
-                    for copy in home(p):
-                        copy.start()
+                for h in range(2):
+                    back(k, p, h).wait_recv()
+                    rs[k, p, halves[h], :] = (
+                        own[k, p, halves[h], :] + ret[k, p, halves[h], :].astype(F32)
+                    ).astype(BF16)
+
+                    @pl.when(k < s - 1)
+                    def _():
+                        back(k, p, h).start()
+
+                    @pl.when(k == s - 1)
+                    def _():
+                        home(s - 1, p, h).start()
 
             return carry
 
@@ -350,7 +359,8 @@
 
         @pl.when(jnp.logical_not(last))
         def _():
-            home_arrived(p)
+            for h in range(2):
+                home(s, p, h).wait_recv()
             out[:, mine] = (own[s, p, here, :] + ret[s, p, here, :].astype(F32)).astype(BF16)
             out[:, theirs] = (finr[p] + retd[p].astype(F32)).astype(BF16)
 
@@ -367,17 +377,16 @@
         lax.fori_loop(0, s + 1, body, 0)
 
     def drain(k, carry):
-        for p in range(2):
-            back(k, p).wait_send()
+        for p, h in pieces4:
+            back(k, p, h).wait_send()
         return carry
 
-    lax.fori_loop(0, s - 1, drain, 0)
+    lax.fori_loop(jnp.where(last, jnp.maximum(s - 2, 0), 0), s - 1, drain, 0)
 
     @pl.when(s >= 1)
     def _():
-        for p in range(2):
-            for copy in home(p):
-                copy.wait_send()
+        for p, h in pieces4:
+            home(s - 1, p, h).wait_send()
 
 
 def hand_over(a, b, c, x, y, z):
@@ -430,7 +439,7 @@
             pltpu.VMEM((2, rows, hs), F32),
             dma((4 * PARTS,)), dma((4 + PARTS,)),
             *[dma((PARTS,))] * 6,
-            dma((stages, 2)), dma((stages, 2)), dma((stages, 2)), dma((stages, 2)), dma((2,)), dma((2,)),
+            dma((stages, 2)), dma((stages, 2)), dma((stages, 4)), dma((stages, 4)), dma((2,)), dma((2,)),
             dma((4,)), dma((4,)), dma((2,)), dma((2,)),
         ],
         compiler_params=pltpu.CompilerParams(

time: 39.1 us -> 38.5 us (0.985)
  Pallas kernels: 38.3 us -> 37.7 us
    pallas_call x1, Pallas kernels: 36.5 us -> 36 us  [per_device(): pl.pallas_call(functools.partial(kernel, stages), out_shape=(jax.ShapeDty...]
where the time goes in v6:
time: 38.5 us; the launch traced here: 38.3 us
  Pallas kernels  37.7 us (98%)
  between operations  0.64 us (2%)
    pallas_call x1, Pallas kernels, per_device(): pl.pallas_call(functools.partial(kernel, stages), out_shape=(jax.ShapeDty...  36 us
    pallas_call x1, Pallas kernels, per_device(): pl.pallas_call(hand_over, out_shape=tuple((jax.ShapeDtypeStruct(a.shape,...  1.73 us

profile of v6, /device:TPU:0, one launch (start us, length us, event | category | flops | bytes accessed | tf_op | source)
XLA Modules:
  0.0 38.3 jit_solution(2183661113652079829)
XLA Ops:
  0.6 36.0 %attention_backward.1 = (bf16[128,1024]{1,0:T(8,128)(2,1)}, bf16[128,256]{1,0:T(8,128)(2,1)}, bf16[128,256]{1,0:T(8,128)(2,1)}) custom-call(bf16[128,1024]{1,0:T(8,128)(2,1)} %q_in.1, bf16[128,256]{1,0:T(8,128)(2,1)} %k_hbm.1, bf16[128,256]{1,0:T(8,128)(2,1)} %v_hbm.1, bf16[128,1024]{1,0:T(8,128)(2,1)} %g_in.1, bf16[4096,1024]{1,0:T(8,128)(2,1)} %w_hbm.1, ...), custom_call_target="tpu_custom_call" | custom-call | tf_op jit(solution)/shard_map/attention_backward/pallas_call | solution.py:404
  36.6 1.7 %hand_over.1 = (bf16[128,1024]{1,0:T(8,128)(2,1)}, bf16[128,256]{1,0:T(8,128)(2,1)}, bf16[128,256]{1,0:T(8,128)(2,1)}) custom-call(bf16[128,1024]{1,0:T(8,128)(2,1)} %get-tuple-element.6.a, bf16[128,256]{1,0:T(8,128)(2,1)} %get-tuple-element.7.b, bf16[128,256]{1,0:T(8,128)(2,1)} %get-tuple-element.8.c), custom_call_target="tpu_custom_call" | custom-call | tf_op jit(solution)/shard_map/hand_over/pallas_call | solution.py:450

commit v7 on v6

--- a/solution.py
+++ b/solution.py
@@ -266,24 +266,26 @@
 
     fin = [remote(fins.at[p], finr.at[p], fin_s.at[p], fin_r.at[p], sib) for p in range(2)]
 
+    def stacked(ref):
+        return jnp.concatenate([heads(ref, r) for r in range(RATIO)], 0)
+
     def gradients(k, carry):
         if keep:
             keys, values = pieces(k)
         else:
             keys, values, allowed = block(k)
         turned = keys.T
-        dk = jnp.zeros((pair, hs), F32)
-        dv = jnp.zeros((pair, hs), F32)
+        probs_low, dscores_low = [], []
         for r in range(RATIO):
             sc = kept[k, r] if keep else scores(keys, allowed, r)
             dp = dot(values, heads(ubuf, r), 1, 1)
             pr = jnp.exp2(sc - mst[r : r + 1, :])
             ds = (pr * (dp - wst[r : r + 1, :])).astype(BF16)
-            dv += dot(pr.astype(BF16), heads(ubuf, r), 1, 0)
-            dk += dot(ds, heads(qbuf, r), 1, 0)
+            probs_low.append(pr.astype(BF16))
+            dscores_low.append(ds)
             dq[r] += dot(turned, ds, 1, 0)
-        own[k, 0] = dk * scale
-        own[k, 1] = dv
+        own[k, 0] = dot(jnp.concatenate(dscores_low, 1), stacked(qbuf), 1, 0) * scale
+        own[k, 1] = dot(jnp.concatenate(probs_low, 1), stacked(ubuf), 1, 0)
 
         @pl.when(last & (k < s))
         def _():

time: 38.5 us -> 38.8 us (level)
  no operation moved by 1% of the time
where the time goes in v7:
time: 38.8 us; the launch traced here: 38.6 us
  Pallas kernels  38 us (98%)
  between operations  0.64 us (2%)
    pallas_call x1, Pallas kernels, per_device(): pl.pallas_call(functools.partial(kernel, stages), out_shape=(jax.ShapeDty...  36.2 us
    pallas_call x1, Pallas kernels, per_device(): pl.pallas_call(hand_over, out_shape=tuple((jax.ShapeDtypeStruct(a.shape,...  1.73 us

profile of v7, /device:TPU:0, one launch (start us, length us, event | category | flops | bytes accessed | tf_op | source)
XLA Modules:
  0.0 38.6 jit_solution(1339215468699981636)
XLA Ops:
  0.6 36.2 %attention_backward.1 = (bf16[128,1024]{1,0:T(8,128)(2,1)}, bf16[128,256]{1,0:T(8,128)(2,1)}, bf16[128,256]{1,0:T(8,128)(2,1)}) custom-call(bf16[128,1024]{1,0:T(8,128)(2,1)} %q_in.1, bf16[128,256]{1,0:T(8,128)(2,1)} %k_hbm.1, bf16[128,256]{1,0:T(8,128)(2,1)} %v_hbm.1, bf16[128,1024]{1,0:T(8,128)(2,1)} %g_in.1, bf16[4096,1024]{1,0:T(8,128)(2,1)} %w_hbm.1, ...), custom_call_target="tpu_custom_call" | custom-call | tf_op jit(solution)/shard_map/attention_backward/pallas_call | solution.py:406
  36.9 1.7 %hand_over.1 = (bf16[128,1024]{1,0:T(8,128)(2,1)}, bf16[128,256]{1,0:T(8,128)(2,1)}, bf16[128,256]{1,0:T(8,128)(2,1)}) custom-call(bf16[128,1024]{1,0:T(8,128)(2,1)} %get-tuple-element.6.a, bf16[128,256]{1,0:T(8,128)(2,1)} %get-tuple-element.7.b, bf16[128,256]{1,0:T(8,128)(2,1)} %get-tuple-element.8.c), custom_call_target="tpu_custom_call" | custom-call | tf_op jit(solution)/shard_map/hand_over/pallas_call | solution.py:452
